TPU v7x, 32 devices: a whole 2x2x4 slice. The times are simulated.
32 devices in a mesh: shard: 4 (over y, core), replica: 8 (over z, x).
Axes of the slice: x: 2, y: 2, z: 4, core: 2. Of those that a mesh axis runs over, the one named last changes fastest.
Arguments:
- tokens: bfloat16 [256, 129, 1024], P(('shard', 'replica')), may hold values from -6 to 6
- norm1_gain: bfloat16 [1024], P('shard'), may hold values from 0.099609375 to 1.8984375
- norm1_shift: bfloat16 [1024], P('shard'), may hold values from -3 to 3
- w_qkv: bfloat16 [1024, 3072], P('shard'), may hold values from -0.1875 to 0.1875
- bias_qv: bfloat16 [2048], P('shard'), may hold values from -3 to 3
- w_out: bfloat16 [1024, 1024], P('shard'), may hold values from -0.75 to 0.75
- bias_out: bfloat16 [1024], P('shard'), may hold values from -3 to 3
- scale_one: bfloat16 [1024], P('shard'), may hold values from 0.5 to 1.5
- norm2_gain: bfloat16 [1024], P('shard'), may hold values from 0.099609375 to 1.8984375
- norm2_shift: bfloat16 [1024], P('shard'), may hold values from -3 to 3
- w_up: bfloat16 [1024, 4096], P(None, 'shard'), may hold values from -0.1875 to 0.1875
- bias_up: bfloat16 [4096], P('shard'), may hold values from -3 to 3
- w_down: bfloat16 [4096, 1024], P('shard'), may hold values from -0.09375 to 0.09375
- bias_down: bfloat16 [1024], P('shard'), may hold values from -3 to 3
- scale_two: bfloat16 [1024], P('shard'), may hold values from 0.5 to 1.5
- cotangent: bfloat16 [256, 129, 1024], P(('shard', 'replica')), may hold values from -6 to 6
Outputs:
- result: bfloat16 [256, 129, 1024], P(('shard', 'replica'))
- grad_tokens: bfloat16 [256, 129, 1024], P(('shard', 'replica'))
- grad_norm1_gain: float32 [1024], P('shard')
- grad_norm1_shift: float32 [1024], P('shard')
- grad_w_qkv: float32 [1024, 3072], P('shard')
- grad_bias_qv: float32 [2048], P('shard')
- grad_w_out: float32 [1024, 1024], P('shard')
- grad_bias_out: float32 [1024], P('shard')
- grad_scale_one: float32 [1024], P('shard')
- grad_norm2_gain: float32 [1024], P('shard')
- grad_norm2_shift: float32 [1024], P('shard')
- grad_w_up: float32 [1024, 4096], P(None, 'shard')
- grad_bias_up: float32 [4096], P('shard')
- grad_w_down: float32 [4096, 1024], P('shard')
- grad_bias_down: float32 [1024], P('shard')
- grad_scale_two: float32 [1024], P('shard')
All inputs are finite; a program needn't handle non-finite values.
Results may differ from a plain program's by a relative error of at most 0.02.
Values may be sent and summed in bfloat16 or wider, within the bound.
A program may use at most 320 MiB of HBM per device.

v0:
```python
import functools

import jax
import jax.numpy as jnp
from jax import lax
from jax.experimental import pallas as pl
from jax.experimental.pallas import tpu as pltpu
from jax.sharding import PartitionSpec as P

F32 = jnp.float32
BF16 = jnp.bfloat16
D = 1024
FF = 4096
HEADS = 16
PATCH = 128
CLS = 16
TILE = 512
FACTOR = 0.125
MESH = pl.DeviceIdType.MESH


def dot(a, b):
    return jnp.dot(a, b, preferred_element_type=F32)


def dot_nt(a, b):
    return lax.dot_general(a, b, (((1,), (1,)), ((), ())), preferred_element_type=F32)


def dot_tn(a, b):
    return lax.dot_general(a, b, (((0,), (0,)), ((), ())), preferred_element_type=F32)


def at(index, size):
    return pl.ds(pl.multiple_of(index * size, size), size)


def head_mask():
    lane = lax.shift_right_logical(lax.broadcasted_iota(jnp.int32, (HEADS, D), 1), 6)
    return lane == lax.broadcasted_iota(jnp.int32, (HEADS, D), 0)


def split_pair(v):
    low = lax.broadcasted_iota(jnp.int32, v.shape, 1) < 64
    zero = jnp.zeros_like(v)
    return jnp.concatenate([jnp.where(low, v, zero), jnp.where(low, zero, v)], 0)


def merge_pair(v):
    n = v.shape[0] // 2
    low = lax.broadcasted_iota(jnp.int32, (n, v.shape[1]), 1) < 64
    return jnp.where(low, v[:n], v[n:])


def place():
    s = lax.axis_index("shard")
    r = lax.axis_index("replica")
    x = lax.rem(r, 2)
    z = lax.div(r, 2)
    return s, r, x, z


def peers(s, r):
    sib = s + 1 - 2 * lax.rem(s, 2)
    across = lax.rem(s + 2, 4)
    side = r + 1 - 2 * lax.rem(r, 2)
    return sib, across, side


def rows_loop(n, step, body):
    lax.fori_loop(0, n // step, lambda k, c: (body(at(k, step)), c)[1], 0, unroll=13)


def unpack_vectors(vec, vecf, bias_qkv):
    for v in range(8):
        for s in range(4):
            vecf[v : v + 1, s * 256 : (s + 1) * 256] = vec[s, v : v + 1, :].astype(F32)
    bias_qkv[...] = jnp.zeros_like(bias_qkv)
    for s in range(4):
        for t in range(2):
            col = (s * 2 + t) * 256 + (D if s >= 2 else 0)
            bias_qkv[0:1, col : col + 256] = vec[s, 8 + t : 9 + t, :].astype(F32)


def layer_norm(v, gain, shift):
    c = v - jnp.mean(v, axis=-1, keepdims=True)
    inv = lax.rsqrt(jnp.mean(c * c, axis=-1, keepdims=True) + 1e-06)
    return c * inv * gain + shift


def to_images(src, dst, turn):
    images = (src.shape[0]) // (PATCH + 1)
    main = images * PATCH

    def lane_block(l, carry):
        cols = at(l, 128)
        slot = lax.rem(l, 2)
        turn[slot] = src[0:main, cols].astype(F32)
        for i in range(images):
            dst[i * PATCH : (i + 1) * PATCH, cols] = turn[slot, pl.ds(i, PATCH, stride=images), :].astype(BF16)
        return carry

    lax.fori_loop(0, D // 128, lane_block, 0)
    last = src[main : main + images, :].astype(F32)
    dst[main:, :] = jnp.concatenate([last, jnp.zeros((CLS - images, D), F32)], 0).astype(BF16)


def pack_vectors(vectors, dst):
    row = 0
    for v in vectors:
        count = v.shape[0] // 256
        wide = v[...].astype(F32)
        for k in range(count):
            dst[row : row + 1, :] = wide[k * 256 : (k + 1) * 256].reshape(1, 256)
            row += 1


def attend(i, qkv, qkv_cls, scores, probs, mix, probs_cls, att, att_cls, lse, lse_cls):
    rows = at(i, PATCH)
    mask = head_mask()
    own = qkv_cls[pl.ds(i, 1), :]
    q_c, k_c, v_c = own[:, :D] * FACTOR, own[:, D : 2 * D], own[:, 2 * D :]
    q_bd = jnp.where(mask, q_c, 0.0)
    k_bd = jnp.where(mask, k_c, 0.0).astype(BF16)
    v_bd = jnp.where(mask, v_c, 0.0).astype(BF16)
    to_cls = dot_nt(k_bd, qkv[rows, 0:D]) * FACTOR
    of_cls = dot_nt(q_bd.astype(BF16), qkv[rows, D : 2 * D])
    corner = jnp.sum(q_bd * k_c, axis=1, keepdims=True)
    top = jnp.maximum(jnp.max(of_cls, axis=1, keepdims=True), corner)
    e_row = jnp.exp(of_cls - top)
    e_cor = jnp.exp(corner - top)
    total = jnp.sum(e_row, axis=1, keepdims=True) + e_cor
    inv = 1.0 / total
    row = dot((e_row * inv).astype(BF16), qkv[rows, 2 * D : 3 * D])
    row = row + (e_cor * inv).astype(BF16).astype(F32) * v_c
    att_cls[pl.ds(i, 1), :] = jnp.sum(jnp.where(mask, row, 0.0), axis=0, keepdims=True)
    lse_cls[i] = jnp.broadcast_to(top + jnp.log(total), (HEADS, PATCH))
    for g in range(HEADS // 2):
        q2 = qkv[rows, g * 128 : g * 128 + 128] * jnp.asarray(FACTOR, BF16)
        scores[g] = dot_nt(split_pair(qkv[rows, g * 128 + D : g * 128 + D + 128]), q2)
    for g in range(HEADS // 2):
        for u in range(2):
            h = 2 * g + u
            part = scores[g, u * PATCH : (u + 1) * PATCH, :]
            extra = to_cls[h : h + 1, :]
            top = jnp.maximum(jnp.max(part, axis=0, keepdims=True), extra)
            e_part = jnp.exp(part - top)
            e_extra = jnp.exp(extra - top)
            total = jnp.sum(e_part, axis=0, keepdims=True) + e_extra
            inv = 1.0 / total
            probs[g, u * PATCH : (u + 1) * PATCH, :] = (e_part * inv).astype(BF16)
            probs_cls[h : h + 1, :] = e_extra * inv
            lse[i, h : h + 1, :] = top + jnp.log(total)
    for g in range(HEADS // 2):
        v2 = split_pair(qkv[rows, g * 128 + 2 * D : g * 128 + 2 * D + 128])
        mix[:, g * 128 : g * 128 + 128] = dot_tn(probs[g], v2)
    att[rows, :] = (mix[...] + dot_tn(probs_cls[...].astype(BF16), v_bd)).astype(BF16)


class Gather:
    KINDS = ("own", "far", "x1", "z1", "x2", "z2", "p0", "p1", "p2", "p3", "p4")

    def __init__(self, number, rows, src, dst, sems, local):
        s, r, x, z = place()
        sib, across, side = peers(s, r)
        self.number, self.sems = number, sems
        near = lax.rem(z, 2)
        level = {"replica": (z + 1 - 2 * near) * 2 + x}
        side, sib = {"replica": side}, {"shard": sib}
        size = rows // 4
        half = size // 2

        def start(zz, xx):
            return pl.multiple_of((2 * zz + xx) * size, 16)

        def same(first, count, to):
            ref = dst(across, pl.multiple_of(first, 16), count)
            return ref, ref, to

        mine, by_x, by_z, by_both = start(near, x), start(near, 1 - x), start(1 - near, x), start(1 - near, 1 - x)
        self.parts = {
            "own": (dst(s, 0, rows), dst(s, 0, rows), sib),
            "far": (dst(s, mine, size), dst(s, mine, size), {"shard": across}),
            "x1": same(mine, size, side),
            "z1": same(mine, size, level),
            "x2": same(by_z, half, side),
            "z2": same(by_x + half, half, level),
            "p0": same(mine, size, sib),
            "p1": same(by_x, size, sib),
            "p2": same(by_z, size, sib),
            "p3": same(by_both, half, sib),
            "p4": same(by_both + half, half, sib),
        }
        self.local = pltpu.make_async_copy(src(0, rows), dst(s, 0, rows), local.at[number])

    def copy(self, kind):
        a, b, to = self.parts[kind]
        k = self.KINDS.index(kind)
        return pltpu.make_async_remote_copy(
            a, b, self.sems.at[0, self.number, k], self.sems.at[1, self.number, k], device_id=to, device_id_type=MESH
        )

    def load(self):
        self.local.start()

    def begin(self):
        self.local.wait()
        self.copy("far").start()

    def share(self):
        self.copy("own").start()

    def on_far(self):
        self.copy("far").wait_recv()
        for kind in ("x1", "z1", "p0"):
            self.copy(kind).start()

    def on_near(self):
        self.copy("x1").wait_recv()
        self.copy("z2").start()
        self.copy("p1").start()
        self.copy("z1").wait_recv()
        self.copy("x2").start()
        self.copy("p2").start()

    def on_last(self):
        self.copy("x2").wait_recv()
        self.copy("p3").start()
        self.copy("z2").wait_recv()
        self.copy("p4").start()

    def ready(self):
        for kind in ("own", "p0", "p1", "p2", "p3", "p4"):
            self.copy(kind).wait_recv()

    def drain(self):
        for kind in self.KINDS:
            self.copy(kind).wait_send()


def relative_piece(s, rel):
    low, high = lax.rem(rel, 2), lax.div(rel, 2)
    return s + low * (1 - 2 * lax.rem(s, 2)) + high * (2 - 4 * lax.div(s, 2))


def unpack_bias_up(vec, bias_up):
    for p in range(4):
        for t in range(2):
            for k in range(2):
                row = 10 + 2 * t + k
                bias_up[2 * p + t : 2 * p + t + 1, k * 256 : (k + 1) * 256] = vec[p, row : row + 1, :].astype(F32)


def ffn_tile(act2, dr, dr_t, act2_t, w_up, w_down, bias, hid, br, gmid, fresh, on_back, on_hidden, put):
    n = act2.shape[0]
    cut = 16 * (n // 32)
    first, second = slice(0, cut), slice(cut, n)

    def both(rows, before, grad):
        hidden, step = gelu_both(before)
        hid[rows, :] = hidden.astype(BF16)
        grad = grad * step
        br[rows, :] = grad.astype(BF16)
        return jnp.sum(grad, axis=0, keepdims=True)

    def back(rows):
        out = dot_nt(br[rows, :], w_up())
        if fresh:
            gmid[rows, :] = out
        else:
            gmid[rows, :] += out

    before0 = dot(act2[first, :], w_up()) + bias
    grad0 = dot_nt(dr[first, :], w_down())
    before1 = dot(act2[second, :], w_up()) + bias
    column = both(first, before0, grad0)
    grad1 = dot_nt(dr[second, :], w_down())
    on_back()
    back(first)
    column = column + both(second, before1, grad1)
    back(second)
    on_hidden()
    put(0, dot(dr_t[...], hid[...]).astype(BF16))
    put(1, dot(act2_t[...], br[...]).astype(BF16))
    return column


def gather_kernel(
    tokens, cot, v0, v1, v2, v3, v4, v5, v6, v7, v8, v9, w_qkv, w_out, w_up, w_down,
    qkv_w_o, out_w_o, up_w_o, down_w_o, vec_all, qkv_o, act_t_o, x_o, att_t_o, mid_o, branch_o, act2_o, act2_t_o, up_o,
    dr_o, dr_t_o, lse_o, lsec_o, parts_o, hid_o, gact_o, column_o,
    full_qkv, full_out, full_up, full_down, x_s, qkv, act, att, mid, branch, act2, turned_a, turned_b, lse, lsec,
    scores, probs, mix, probs_cls, cls, qkv_cls, turn, vec32, vec_own_s, vec, vecf, bias_qkv,
    bias_up, column,
    sems, local, vsem, osem,
):
    s, r, x, z = place()
    sib, across, side = peers(s, r)
    n = x_s.shape[0]
    images = lse.shape[0]
    main = images * PATCH

    vec32[...] = jnp.zeros_like(vec32)
    pack_vectors((v0, v1, v2, v3, v4, v5, v6, v7, v8, v9), vec32)
    vec_own_s[...] = vec32[...].astype(BF16)
    barrier = pltpu.get_barrier_semaphore()
    level = (z + 1 - 2 * lax.rem(z, 2)) * 2 + x
    for to in ({"shard": sib}, {"shard": across}, {"replica": side}, {"replica": level}):
        pl.semaphore_signal(barrier, inc=1, device_id=to, device_id_type=MESH)

    def unit(number, rows, src, dst):
        return Gather(number, rows, src, dst, sems, local)

    def qkv_unit(number, t):
        cols = pl.ds(t * 3 * TILE, 3 * TILE)
        return unit(number, 256, lambda a, k: w_qkv.at[pl.ds(a, k), cols],
                    lambda p, a, k: full_qkv.at[pl.ds(pl.multiple_of(p * 256 + a, 16), k), cols])

    g_qa, g_qb = qkv_unit(0, 0), qkv_unit(6, 1)
    g_out = unit(1, 256, lambda a, k: w_out.at[pl.ds(a, k), :],
                 lambda p, a, k: full_out.at[pl.ds(pl.multiple_of(p * 256 + a, 16), k), :])

    def up_unit(number, t):
        cols = pl.ds(t * TILE, TILE)
        return unit(number, D, lambda a, k: w_up.at[pl.ds(a, k), cols],
                    lambda p, a, k: full_up.at[p, pl.ds(pl.multiple_of(a, 16), k), cols])

    def down_unit(number, t):
        return unit(number, TILE, lambda a, k: w_down.at[pl.ds(a + t * TILE, k), :],
                    lambda p, a, k: full_down.at[p, pl.ds(pl.multiple_of(a + t * TILE, 16), k), :])

    g_up0, g_down0, g_up1, g_down1 = up_unit(2, 0), down_unit(3, 0), up_unit(4, 1), down_unit(5, 1)

    for g in (g_qa, g_qb, g_out, g_up0, g_down0, g_up1, g_down1):
        g.load()
    pl.semaphore_wait(barrier, 4)

    def vec_copy(k, src, slot, to):
        return pltpu.make_async_remote_copy(src, vec.at[slot], vsem.at[0, k], vsem.at[1, k], device_id=to,
                                            device_id_type=MESH)

    vec_own = vec_copy(0, vec_own_s, s, {"shard": sib})
    vec_far = vec_copy(1, vec_own_s, s, {"shard": across})
    vec_pass = vec_copy(2, vec.at[across], across, {"shard": sib})
    vec_own.start()
    vec_far.start()
    for g in (g_qa, g_qb):
        g.begin()
        g.share()
    g_out.begin()
    vec[s] = vec_own_s[...]

    to_images(tokens, x_s, turn)
    outs = {}

    def send_out(k, src, dst):
        outs[k] = pltpu.make_async_copy(src, dst, osem.at[k])
        outs[k].start()

    send_out(0, x_s, x_o)
    vec_far.wait_recv()
    vec_pass.start()
    vec_own.wait_recv()
    vec_pass.wait_recv()
    unpack_vectors(vec, vecf, bias_qkv)
    g_qa.on_far()

    def first_norm(rows):
        act[rows, :] = layer_norm(x_s[rows, :].astype(F32), vecf[0:1, :], vecf[1:2, :]).astype(BF16)

    rows_loop(n, 16, first_norm)
    g_qa.on_near()
    g_qb.on_far()
    for g in (g_up0, g_down0, g_up1, g_down1):
        g.begin()
    transpose_into(act, turned_b)
    send_out(1, turned_b, act_t_o)
    to_images(cot, branch, turn)
    g_qa.on_last()
    g_qb.on_near()

    def down_rows(rows):
        act2[rows, :] = (branch[rows, :].astype(F32) * vecf[7:8, :]).astype(BF16)

    rows_loop(n, 16, down_rows)
    send_out(14, branch, up_o)
    send_out(15, act2, dr_o)
    transpose_into(act2, turned_a)
    send_out(16, turned_a, dr_t_o)
    g_qb.on_last()
    g_out.on_far()
    g_qa.ready()

    def qkv_tile(j, carry):
        cols = at(j, TILE)
        low = (dot(act[...], full_qkv[:, cols]) + bias_qkv[0:1, cols]).astype(BF16)
        qkv[:, cols] = low
        qkv_cls[:, cols] = low[main:].astype(F32)
        return carry

    lax.fori_loop(0, 3, qkv_tile, 0)
    g_out.on_near()
    g_qb.ready()
    send_out(4, full_qkv, qkv_w_o)
    for g in (g_out, g_up0, g_down0):
        g.share()
    lax.fori_loop(3, 6, qkv_tile, 0)
    send_out(2, qkv, qkv_o)
    act[...] = act2[...]
    unpack_bias_up(vec, bias_up)
    column[...] = jnp.zeros_like(column)
    send_out(3, vec, vec_all)
    cls[...] = jnp.zeros_like(cls)
    g_out.on_last()
    g_up0.on_far()
    plan = {1: [g_up0.on_near], 2: [g_down0.on_far], 3: [g_up0.on_last, g_up1.share], 4: [g_down0.on_near, g_up1.on_far],
            6: [g_down0.on_last, g_down1.share], 7: [g_up1.on_near, g_down1.on_far]}

    def image(i, carry):
        for k, steps in plan.items():
            @pl.when(i == k)
            def _(steps=steps):
                for step in steps:
                    step()

        attend(i, qkv, qkv_cls, scores, probs, mix, probs_cls, att, cls, lse, lsec)
        return carry

    lax.fori_loop(0, images, image, 0)
    att[main:, :] = cls[...].astype(BF16)
    outs.pop(1).wait()
    transpose_into(att, turned_b)
    send_out(8, turned_b, att_t_o)
    send_out(9, lse, lse_o)
    send_out(10, lsec, lsec_o)
    g_out.ready()
    outs.pop(14).wait()
    for j in range(D // TILE):
        cols = slice(j * TILE, (j + 1) * TILE)
        out = dot(att[...], full_out[:, cols]) + vecf[2:3, cols]
        branch[:, cols] = out.astype(BF16)
        mid[:, cols] = x_s[:, cols].astype(F32) + vecf[3:4, cols] * out
    send_out(11, mid, mid_o)
    send_out(12, branch, branch_o)
    g_up1.on_last()
    g_down1.on_near()

    def second_norm(rows):
        act2[rows, :] = layer_norm(mid[rows, :], vecf[4:5, :], vecf[5:6, :]).astype(BF16)

    outs.pop(15).wait()
    rows_loop(n, 16, second_norm)
    send_out(13, act2, act2_o)
    outs.pop(8).wait()
    transpose_into(act2, turned_b)
    send_out(17, turned_b, act2_t_o)
    half = pl.ds(0, TILE)
    rest = pl.ds(TILE, TILE)
    send_out(5, full_out, out_w_o)
    g_up0.ready()
    send_out(18, full_up.at[:, :, half], up_w_o.at[:, :, half])
    g_down0.ready()
    send_out(19, full_down.at[:, half, :], down_w_o.at[:, half, :])
    for k in (2, 11):
        outs.pop(k).wait()
    hid, br = qkv.at[:, pl.ds(0, TILE)], qkv.at[:, pl.ds(TILE, TILE)]
    for k, rel in enumerate((3, 2)):
        piece = relative_piece(s, rel)

        def put(half_k, value, k=k):
            qkv[0:D, (2 + 2 * k + half_k) * TILE : (3 + 2 * k + half_k) * TILE] = value

        if k:
            outs.pop(22).wait()
        column[pl.ds(2 * piece, 1), :] = ffn_tile(
            act2, act, turned_a, turned_b, lambda: full_up[piece, :, 0:TILE], lambda: full_down[piece, 0:TILE, :],
            bias_up[pl.ds(2 * piece, 1), :], hid, br, mid, k == 0, lambda: None, lambda: send_out(22 + k, hid, hid_o.at[k]), put)
        for half_k in range(2):
            send_out(24 + 2 * k + half_k, qkv.at[pl.ds(0, D), pl.ds((2 + 2 * k + half_k) * TILE, TILE)],
                     parts_o.at[k, pl.ds(half_k * D, D), :])
        if k == 0:
            g_down1.on_last()
            g_up1.ready()
            send_out(20, full_up.at[:, :, rest], up_w_o.at[:, :, rest])
    send_out(28, mid, gact_o)
    send_out(29, column, column_o)
    g_down1.ready()
    send_out(21, full_down.at[:, rest, :], down_w_o.at[:, rest, :])
    for copy in outs.values():
        copy.wait()
    for g in (g_qa, g_qb, g_out, g_up0, g_down0, g_up1, g_down1):
        g.drain()
    for copy in (vec_own, vec_far, vec_pass):
        copy.wait_send()


class Chunk:
    def __init__(self, index, rows, mine, y_send, y_recv, x_recv, z_recv, far):
        self.index, self.rows, self.mine, self.y_send, self.far = index, rows, mine, y_send, far
        self.y_recv, self.x_recv, self.z_recv = y_recv, x_recv, z_recv


def chunk_layout(nz):
    sizes = [1024, 1024, 1024, 1024, 512, 512, 512, 512]
    y_base = 2048
    y_a = y_base
    y_b = y_a + 2048
    mine_base = y_b + 2048
    chunks = []
    mine = mine_base
    late = 0
    xr = zr = 0
    for k, rows in enumerate(sizes):
        if k < 2:
            ys, yr = y_a + 1024 * k, 1024 * k
        elif k < 4:
            ys, yr = y_b + 1024 * (k - 2), 2048 + 1024 * (k - 2)
        else:
            ys, yr = y_a + late, late
            late += rows
        far = mine_base + sum(sizes) + 512 * k if k < 2 else ys
        chunks.append(Chunk(k, rows, mine, ys, yr, xr, zr, far))
        mine += rows
        xr += rows // 2
        zr += rows // 2 // nz
    return chunks, dict(buf=mine + 1024, total=sum(sizes), mine=mine_base, y_recv=2 * 2048, x_recv=xr, z_recv=zr)


def add_rows(dst, d0, src, s0, rows):
    step = next(k for k in (128, 96, 64, 32, 16) if rows % k == 0)

    def body(k, carry):
        d = pl.ds(pl.multiple_of(d0 + k * step, 16), step)
        t = pl.ds(pl.multiple_of(s0 + k * step, 16), step)
        dst[d, :] = (dst[d, :].astype(F32) + src[t, :].astype(F32)).astype(BF16)
        return carry

    lax.fori_loop(0, rows // step, body, 0)


class Reduce:
    def __init__(self, nz, buf, core_recv, y_recv, x_recv, z_recv, sems, core_sems, credit):
        self.nz, self.buf, self.core_recv = nz, buf, core_recv
        self.y_recv, self.x_recv, self.z_recv = y_recv, x_recv, z_recv
        self.sems, self.core_sems, self.credit = sems, core_sems, credit
        self.s, self.r, self.x, self.z = place()
        self.sib, self.across, self.side = peers(self.s, self.r)

    def remote(self, src, dst, chunk, kind, to):
        return pltpu.make_async_remote_copy(
            src, dst, self.sems.at[0, chunk.index, kind], self.sems.at[1, chunk.index, kind], device_id=to,
            device_id_type=MESH)

    def peer(self, k):
        return {"replica": lax.rem(self.z + k, self.nz) * 2 + self.x}

    def core_copy(self, turn, rows):
        slot = turn % 2
        return pltpu.make_async_remote_copy(
            self.buf.at[pl.ds(slot * 1024 if turn > 3 else 0, rows), :], self.core_recv.at[slot, pl.ds(0, rows), :],
            self.core_sems.at[0, turn], self.core_sems.at[1, turn], device_id={"shard": self.sib}, device_id_type=MESH)

    def add_core(self, turn, first, dst, rows):
        add_rows(self.buf, dst, self.core_recv.at[turn % 2], first, rows)

    def y_copy(self, c):
        return self.remote(self.buf.at[pl.ds(c.y_send, c.rows), :], self.y_recv.at[pl.ds(c.y_recv, c.rows), :], c, 0,
                           {"shard": self.across})

    def x_copy(self, c):
        half = c.rows // 2
        return self.remote(self.buf.at[pl.ds(pl.multiple_of(c.mine + (1 - self.x) * half, 16), half), :],
                           self.x_recv.at[pl.ds(c.x_recv, half), :], c, 1, {"replica": self.side})

    def quarter(self, c, x, z):
        half = c.rows // 2
        size = half // self.nz
        return pl.ds(pl.multiple_of(c.mine + x * half + z * size, 16), size)

    def z_copy(self, c, k):
        size = c.rows // 2 // self.nz
        return self.remote(self.buf.at[self.quarter(c, self.x, lax.rem(self.z + k, self.nz)), :],
                           self.z_recv.at[k - 1, pl.ds(c.z_recv, size), :], c, 1 + k, self.peer(k))

    def done(self, first, c, z):
        size = c.rows // 2 // self.nz
        return pl.ds(pl.multiple_of(first + z * size, 16), size)

    def back_z(self, c, k):
        part = self.x_recv.at[self.done(c.x_recv, c, self.z), :]
        return self.remote(part, part, c, self.nz + k, self.peer(k))

    def back_x(self, c, k):
        z = lax.rem(self.z + self.nz - k, self.nz)
        return self.remote(self.x_recv.at[self.done(c.x_recv, c, z), :], self.buf.at[self.done(c.far, c, z), :], c,
                           2 * self.nz + k, {"replica": self.side})

    def on_y(self, c):
        self.y_copy(c).wait_recv()
        add_rows(self.buf, c.mine, self.y_recv, c.y_recv, c.rows)
        self.y_copy(c).wait_send()
        self.x_copy(c).start()

    def on_x(self, c):
        half = c.rows // 2
        self.x_copy(c).wait_recv()
        add_rows(self.buf, c.mine + self.x * half, self.x_recv, c.x_recv, half)
        for k in range(1, self.nz):
            self.z_copy(c, k).start()

    def on_z(self, c):
        size = c.rows // 2 // self.nz
        start = c.mine + self.x * (c.rows // 2) + self.z * size
        for k in range(1, self.nz):
            self.z_copy(c, k).wait_recv()
        step = next(k for k in (64, 48, 32, 16) if size % k == 0)

        def body(i, carry):
            d = pl.ds(pl.multiple_of(start + i * step, 16), step)
            total = self.buf[d, :].astype(F32)
            for k in range(1, self.nz):
                total = total + self.z_recv[k - 1, pl.ds(pl.multiple_of(c.z_recv + i * step, 16), step), :].astype(F32)
            to = pl.ds(pl.multiple_of(c.x_recv + self.z * size + i * step, 16), step)
            self.x_recv[to, :] = total.astype(BF16)
            return carry

        lax.fori_loop(0, size // step, body, 0)
        for k in range(1, self.nz):
            self.back_z(c, k).start()
        self.back_x(c, 0).start()

    def on_back(self, c):
        for k in range(1, self.nz):
            self.back_z(c, k).wait_recv()
            self.back_x(c, k).start()

    def finish(self, c):
        for k in range(self.nz):
            self.back_x(c, k).wait_recv()

    def drain(self, c):
        self.x_copy(c).wait_send()
        for k in range(1, self.nz):
            self.z_copy(c, k).wait_send()
            self.back_z(c, k).wait_send()
        for k in range(self.nz):
            self.back_x(c, k).wait_send()


def fold(v):
    return jnp.sum(v.reshape(v.shape[0] // 8, 8, v.shape[1]), axis=0)


def gelu_both(v):
    e = jnp.exp(-0.5 * v * v)
    t = 1.0 / (1.0 + 0.23164189 * jnp.abs(v))
    poly = ((((1.061405429 * t - 1.453152027) * t + 1.421413741) * t - 0.284496736) * t + 0.254829592) * t
    tail = 0.5 * poly * e
    phi = jnp.where(v >= 0.0, 1.0 - tail, tail)
    return v * phi, phi + v * e * 0.3989422804014327


def transpose_into(src, dst):
    for c in range(D // 128):
        dst[c * 128 : (c + 1) * 128, :] = src[:, c * 128 : (c + 1) * 128].T


def attend_back(
    i, qkv, qkv_cls, datt, datt_cls, lse, lsec, scores, dprobs, probs, dscores, cls_row, joint_cls, joint, extra, sum_q, sum_v
):
    rows = at(i, PATCH)
    mask = head_mask()
    own = qkv_cls[pl.ds(i, 1), :]
    do_c = datt_cls[pl.ds(i, 1), :]
    q_c, k_c, v_c = own[:, :D] * FACTOR, own[:, D : 2 * D], own[:, 2 * D :]
    pick = lambda v: jnp.where(mask, v, 0.0)
    q_w, k_w, v_w, do_w = pick(q_c), pick(k_c), pick(v_c), pick(do_c)
    q_bd, k_bd, v_bd, do_bd = (v.astype(BF16) for v in (q_w, k_w, v_w, do_w))
    queries, keys, values = (qkv[rows, k * D : (k + 1) * D] for k in range(3))
    grads = datt[rows, :]
    low = lambda v: v.astype(BF16)
    top = lsec[i][:, 0:1]
    p_row = jnp.exp(dot_nt(q_bd, keys) - top)
    p_cor = jnp.exp(jnp.sum(q_w * k_c, axis=1, keepdims=True) - top)
    dp_row = dot_nt(do_bd, values)
    dp_cor = jnp.sum(do_w * v_c, axis=1, keepdims=True)
    delta = jnp.sum(p_row * dp_row, axis=1, keepdims=True) + p_cor * dp_cor
    ds_row = low(p_row * (dp_row - delta))
    ds_cor = low(p_cor * (dp_cor - delta)).astype(F32)
    p_col = jnp.exp(dot_nt(k_bd, queries) * FACTOR - lse[i])
    dp_col = dot_nt(v_bd, grads)
    for g in range(HEADS // 2):
        lanes = slice(g * 128, (g + 1) * 128)
        q2 = qkv[rows, lanes] * jnp.asarray(FACTOR, BF16)
        scores[g] = dot_nt(split_pair(qkv[rows, g * 128 + D : g * 128 + D + 128]), q2)
        dprobs[g] = dot_nt(split_pair(qkv[rows, g * 128 + 2 * D : g * 128 + 2 * D + 128]), datt[rows, lanes])
    for g in range(HEADS // 2):
        for u in range(2):
            h = 2 * g + u
            half = slice(u * PATCH, (u + 1) * PATCH)
            part = jnp.exp(scores[g, half, :] - lse[i, h : h + 1, :])
            dpart = dprobs[g, half, :]
            p_h, dp_h = p_col[h : h + 1, :], dp_col[h : h + 1, :]
            delta = jnp.sum(part * dpart, axis=0, keepdims=True) + p_h * dp_h
            probs[g, half, :] = low(part)
            dscores[g, half, :] = low(part * (dpart - delta))
            cls_row[h : h + 1, :] = p_h * (dp_h - delta)
    ds_col = low(cls_row[...])
    total = lambda v: jnp.sum(jnp.where(mask, v, 0.0), axis=0, keepdims=True)
    joint_cls[pl.ds(i, 1), 0:D] = FACTOR * (total(dot(ds_row, keys)) + jnp.sum(ds_cor * k_w, axis=0, keepdims=True))
    joint_cls[pl.ds(i, 1), D : 2 * D] = FACTOR * total(dot(ds_col, queries)) + jnp.sum(ds_cor * q_w, axis=0, keepdims=True)
    joint_cls[pl.ds(i, 1), 2 * D : 3 * D] = total(dot(low(p_col), grads)) + jnp.sum(
        low(p_cor).astype(F32) * do_w, axis=0, keepdims=True)
    extra[0] = dot_tn(ds_col, k_bd) * FACTOR
    extra[1] = dot_tn(ds_row, q_bd)
    extra[2] = dot_tn(low(p_row), do_bd)
    for g in range(HEADS // 2):
        lanes = slice(g * 128, (g + 1) * 128)
        klanes = slice(g * 128 + D, g * 128 + D + 128)
        vlanes = slice(g * 128 + 2 * D, g * 128 + 2 * D + 128)
        q2 = qkv[rows, lanes] * jnp.asarray(FACTOR, BF16)
        dv = merge_pair(dot(probs[g], datt[rows, lanes])) + extra[2, :, lanes]
        dk = merge_pair(dot(dscores[g], q2)) + extra[1, :, lanes]
        dq = dot_tn(dscores[g], split_pair(qkv[rows, klanes])) * FACTOR + extra[0, :, lanes]
        joint[:, lanes] = low(dq)
        joint[:, klanes] = low(dk)
        joint[:, vlanes] = low(dv)
        sum_q[:, lanes] += fold(dq)
        sum_v[:, lanes] += fold(dv)
    qkv[rows, :] = joint[...]


def to_tokens(src, dst, turn):
    images = dst.shape[0] // (PATCH + 1)
    main = images * PATCH

    def lane_block(l, carry):
        cols = at(l, 128)
        slot = lax.rem(l, 2)
        for i in range(images):
            turn[slot, pl.ds(i, PATCH, stride=images), :] = src[i * PATCH : (i + 1) * PATCH, cols].astype(F32)
        dst[0:main, cols] = turn[slot].astype(BF16)
        return carry

    lax.fori_loop(0, D // 128, lane_block, 0)
    dst[main : main + images, :] = src[main:, :].astype(F32)[0:images].astype(BF16)


def backward_kernel(
    nz, chunks, vec, full_qkv, full_out, full_up, full_down, qkv_h, act_t_h, x_h, att_t_h, mid_h, branch_h, act2_h,
    act2_t_h, up_h, dr_h, dr_t_h, lse_h, lsec_h, parts_h, hid_h, gact_h, column_h,
    result_o, tokens_o, sums_o, small_o, hidden_o,
    buf, core_recv, y_recv, x_recv, z_recv, gmid, grad_mid, up_s, acc, sums_up, vecf, bias_qkv, bias_up, v_part, v_group, v_sum, v_all,
    sems, core_sems, group_sems, all_sems, credit, dsem, wsem, hsem, osem, fsem,
):
    images = lse_h.shape[0]
    n = gmid.shape[0]
    main = images * PATCH
    red = Reduce(nz, buf, core_recv, y_recv, x_recv, z_recv, sems, core_sems, credit)
    s = red.s
    cd0, cu0, cd1, cu1, co, *cq = chunks

    def load(k, src, dst):
        copy = pltpu.make_async_copy(src, dst, dsem.at[k])
        copy.start()
        return copy

    def relative(rel):
        return relative_piece(s, rel)

    def target(rel, chunk, base):
        low, high = lax.rem(rel, 2), lax.div(rel, 2)
        return low * (base + (1 - high) * chunk.rows) + (1 - low) * (high * chunk.y_send + (1 - high) * chunk.mine)

    def group_peer(k):
        return {"shard": lax.rem(s + k, 4)}

    def replica_peer(k):
        return {"replica": lax.rem(red.r + k, 2 * nz)}

    def group_copy(k):
        return pltpu.make_async_remote_copy(
            v_part.at[lax.rem(s + k, 4)], v_group.at[k - 1], group_sems.at[0, k - 1], group_sems.at[1, k - 1],
            device_id=group_peer(k), device_id_type=MESH)

    def all_copy(k):
        return pltpu.make_async_remote_copy(
            v_sum, v_all.at[red.r], all_sems.at[0, k - 1], all_sems.at[1, k - 1], device_id=replica_peer(k),
            device_id_type=MESH)

    got_up = load(7, up_h, up_s)

    def ffn(dr, dr_t, act2, act2_t, w_up, w_down, hid, br):
        def fetch(j, slot):
            piece, t = relative(3 - lax.rem(j, 4)), lax.div(j, 4)
            return (
                pltpu.make_async_copy(full_up.at[piece, :, at(t, TILE)], w_up.at[slot], wsem.at[0, slot]),
                pltpu.make_async_copy(full_down.at[piece, at(t, TILE), :], w_down.at[slot], wsem.at[1, slot]),
            )

        for copy in fetch(2, 0):
            copy.start()
        got_parts, got_act2, got_dr = (load(8, parts_h.at[0], buf.at[pl.ds(0, 2048), :]), load(0, act2_h, act2),
                                       load(1, dr_h, dr))
        got_gact, got_column = load(10, gact_h, gmid), load(11, column_h, sums_up)
        gots = [got_parts, load(9, parts_h.at[1], buf.at[pl.ds(cd0.y_send, 2048), :]), got_act2, got_dr,
                load(2, dr_t_h, dr_t), load(3, act2_t_h, act2_t), got_gact, got_column]

        def keep(j, slot):
            return pltpu.make_async_copy(hid.at[slot], hidden_o.at[j - 2], hsem.at[slot])

        barrier = pltpu.get_barrier_semaphore()
        partners = [group_peer(k) for k in range(1, 4)] + [replica_peer(k) for k in range(1, 2 * nz)]
        for to in partners:
            pl.semaphore_signal(barrier, inc=1, device_id=to, device_id_type=MESH)
        pl.semaphore_wait(barrier, len(partners))
        unpack_vectors(vec, vecf, bias_qkv)
        unpack_bias_up(vec, bias_up)
        acc[...] = jnp.zeros_like(acc)
        gots[0].wait()
        red.core_copy(0, 2048).start()
        late = gots[4:6]
        for copy in gots[2:4]:
            copy.wait()

        def tile(j, carry):
            slot = lax.rem(j, 2)
            rel, t = 3 - lax.rem(j, 4), lax.div(j, 4)
            piece = relative(rel)
            low, high = lax.rem(rel, 2), lax.div(rel, 2)
            place_at = pl.multiple_of(
                (1 - low) * (high * (cd0.y_send + t * (cd1.y_send - cd0.y_send)) + (1 - high) * (cd0.mine + t * 2048)), 16)
            for copy in fetch(j, slot):
                copy.wait()

            @pl.when(j < 7)
            def _():
                for copy in fetch(j + 1, 1 - slot):
                    copy.start()

            @pl.when(j >= 4)
            def _():
                keep(j - 2, slot).wait()

            for k in (2, 4, 6):
                @pl.when(j == k)
                def _(k=k):
                    red.core_copy(k // 2 - 1, 2048).wait_send()

            def on_back():
                @pl.when(j == 2)
                def _():
                    for copy in gots[1:2] + gots[6:]:
                        copy.wait()

            def on_hidden():
                keep(j, slot).start()

                @pl.when(j == 2)
                def _():
                    for copy in late:
                        copy.wait()

            def put(half, value):
                buf[pl.ds(pl.multiple_of(place_at + half * D, 16), D), :] = value

            sums_up[pl.ds(2 * piece + t, 1), :] = ffn_tile(
                act2, dr, dr_t, act2_t, lambda: w_up[slot], lambda: w_down[slot], bias_up[pl.ds(2 * piece + t, 1), :],
                hid.at[slot], br, gmid, False, on_back, on_hidden, put)

            def y_part(turn, chunk):
                red.core_copy(turn, 2048).wait_recv()
                for k, c in enumerate(chunk):
                    red.add_core(turn, k * 1024, c.y_send, c.rows)
                    red.y_copy(c).start()

            def own_part(turn, chunk):
                red.core_copy(turn, 2048).wait_recv()
                red.add_core(turn, 0, chunk[0].mine, 2048)

            steps = {
                2: [lambda: y_part(0, (cd0, cu0)), lambda: red.core_copy(1, 2048).start()],
                3: [lambda: own_part(1, (cd0, cu0))],
                4: [lambda: red.core_copy(2, 2048).start()],
                5: [lambda: y_part(2, (cd1, cu1)), lambda: red.on_y(cd0)],
                6: [lambda: red.core_copy(3, 2048).start(), lambda: red.on_x(cd0)],
                7: [lambda: own_part(3, (cd1, cu1)), lambda: red.on_y(cu0)],
            }
            for k, todo in steps.items():
                @pl.when(j == k)
                def _(todo=todo):
                    for step in todo:
                        step()
            return carry

        lax.fori_loop(2, 8, tile, 0)
        pl.semaphore_signal(credit, inc=1, device_id={"shard": red.across}, device_id_type=MESH)
        for j in (6, 7):
            keep(j, j % 2).wait()
        red.core_copy(3, 2048).wait_send()

    v = pltpu.VMEM
    pl.run_scoped(ffn, v((n, D), BF16), v((D, n), BF16), v((n, D), BF16), v((D, n), BF16), v((2, D, TILE), BF16),
                  v((2, TILE, D), BF16), v((2, n, TILE), BF16), v((n, TILE), BF16))
    got_up.wait()

    def spread(out, chunk, tile_rows, turn):
        for p in range(4):
            low = lax.rem(lax.rem(s, 2) + p % 2, 2)
            high = lax.rem(lax.div(s, 2) + p // 2, 2)
            start = pl.multiple_of(target(low + 2 * high, chunk, 1024 * (turn % 2)) + tile_rows, 16)
            buf[pl.ds(start, 256), :] = out[p * 256 : (p + 1) * 256].astype(BF16)

    def on_core(turn, chunk):
        red.core_copy(turn, 2 * chunk.rows).wait_recv()
        red.add_core(turn, 0, chunk.y_send, chunk.rows)
        red.y_copy(chunk).start()
        red.add_core(turn, chunk.rows, chunk.mine, chunk.rows)

    def attention(
        qkv, datt, brr, lse, lsec, scores, dprobs, probs, dscores, cls_row, qkv_cls, datt_cls, joint_cls, joint, extra
    ):
        got_qkv, got_lse, got_lsec = load(0, qkv_h, qkv), load(1, lse_h, lse), load(2, lsec_h, lsec)

        def middle(mid, branch, att_t, w_out):
            got_mid, got_branch = load(3, mid_h, mid), load(4, branch_h, branch)
            got_att, got_out = load(5, att_t_h, att_t), load(6, full_out, w_out)
            red.on_z(cd0)
            got_mid.wait()
            got_branch.wait()

            def norm_rows(rows):
                m = mid[rows, :]
                c = m - jnp.mean(m, axis=-1, keepdims=True)
                inv = lax.rsqrt(jnp.mean(c * c, axis=-1, keepdims=True) + 1e-06)
                hat = c * inv
                g = gmid[rows, :]
                acc[4] += fold(g * hat)
                acc[5] += fold(g)
                sc = g * vecf[4:5, :]
                back = inv * (sc - jnp.mean(sc, axis=-1, keepdims=True)
                              - hat * jnp.mean(sc * hat, axis=-1, keepdims=True))
                gm = up_s[rows, :].astype(F32) + back
                grad_mid[rows, :] = gm
                acc[3] += fold(gm * branch[rows, :].astype(F32))
                gb = gm * vecf[3:4, :]
                acc[2] += fold(gb)
                brr[rows, :] = gb.astype(BF16)

            rows_loop(n, 16, norm_rows)
            got_att.wait()
            for q in range(2):
                spread(dot(att_t[...], brr[:, q * TILE : (q + 1) * TILE]), co, q * 256, 4)
            red.core_copy(4, 2 * co.rows).start()
            got_out.wait()
            for q in range(2):
                datt[:, q * TILE : (q + 1) * TILE] = dot_nt(brr[...], w_out[q * TILE : (q + 1) * TILE, :]).astype(BF16)
            red.on_x(cu0)

        pl.run_scoped(middle, v((n, D), F32), v((n, D), BF16), v((D, n), BF16), v((D, D), BF16))
        got_qkv.wait()
        got_lse.wait()
        got_lsec.wait()
        qkv_cls[...] = qkv[main:, :].astype(F32)
        datt_cls[...] = datt[main:, :].astype(F32)
        joint_cls[...] = jnp.zeros_like(joint_cls)
        pl.semaphore_wait(credit, 1)
        on_core(4, co)
        plan = {0: [lambda: red.on_y(cd1), lambda: red.on_back(cd0)], 3: [lambda: red.on_z(cu0)], 5: [lambda: red.on_x(cd1)],
                6: [lambda: red.on_y(cu1), lambda: red.on_back(cu0)]}

        def image(i, carry):
            for k, steps in plan.items():
                @pl.when(i == k)
                def _(steps=steps):
                    for step in steps:
                        step()

            attend_back(i, qkv, qkv_cls, datt, datt_cls, lse, lsec, scores, dprobs, probs, dscores, cls_row, joint_cls,
                        joint, extra, acc.at[8], acc.at[9])
            return carry

        lax.fori_loop(0, images, image, 0)
        qkv[main:, :] = joint_cls[...].astype(BF16)
        acc[8] += fold(joint_cls[:, 0:D])
        acc[9] += fold(joint_cls[:, 2 * D : 3 * D])

        def tail(act_t, w_qkv, turn, flat):
            x_s, gact, new = brr, gmid, datt
            got_act, got_x = load(3, act_t_h, act_t), load(4, x_h, x_s)

            def fetch(j):
                return pltpu.make_async_copy(full_qkv.at[pl.ds(j * 256, 256), :], w_qkv.at[j % 2], wsem.at[0, j % 2])

            fetch(0).start()
            fetch(1).start()
            def weight_grad(k):
                for q in range(2):
                    cols = slice((2 * k + q) * TILE, (2 * k + q + 1) * TILE)
                    spread(dot(act_t[...], qkv[:, cols]), cq[k], q * 256, 5 + k)

            def input_grad(j):
                fetch(j).wait()
                gact[:, j * 256 : (j + 1) * 256] = dot_nt(qkv[...], w_qkv[j % 2])
                if j < 2:
                    fetch(j + 2).start()

            got_act.wait()
            weight_grad(0)
            red.core_copy(5, 1024).start()
            red.on_z(cd1)
            red.core_copy(4, 1024).wait_send()
            weight_grad(1)
            on_core(5, cq[0])
            red.core_copy(6, 1024).start()
            red.on_y(co)
            red.core_copy(5, 1024).wait_send()
            weight_grad(2)
            on_core(6, cq[1])
            red.core_copy(7, 1024).start()
            red.on_x(cu1)
            red.on_back(cd1)
            input_grad(0)
            input_grad(1)
            on_core(7, cq[2])
            red.on_x(co)
            input_grad(2)
            red.on_y(cq[0])
            input_grad(3)
            red.on_z(cu1)
            got_x.wait()

            def norm_rows(rows):
                m = x_s[rows, :].astype(F32)
                c = m - jnp.mean(m, axis=-1, keepdims=True)
                inv = lax.rsqrt(jnp.mean(c * c, axis=-1, keepdims=True) + 1e-06)
                hat = c * inv
                g = gact[rows, :]
                acc[0] += fold(g * hat)
                acc[1] += fold(g)
                sc = g * vecf[0:1, :]
                back = inv * (sc - jnp.mean(sc, axis=-1, keepdims=True)
                              - hat * jnp.mean(sc * hat, axis=-1, keepdims=True))
                new[rows, :] = (grad_mid[rows, :] + back).astype(BF16)

            rows_loop(n, 16, norm_rows)
            red.on_z(co)
            red.on_x(cq[0])
            to_tokens(new, flat, turn)
            copy = pltpu.make_async_copy(flat, tokens_o, osem.at[0])
            copy.start()
            red.on_back(cu1)
            red.on_back(co)
            red.on_y(cq[1])
            copy.wait()

        pl.run_scoped(tail, v((D, n), BF16), v((2, 256, 3 * D), BF16),
                      v((2, main, 128), F32), v((main + images, D), BF16))

    pl.run_scoped(attention, v((n, 3 * D), BF16), v((n, D), BF16), v((n, D), BF16), v((images, HEADS, PATCH), F32),
                  v((images, HEADS, PATCH), F32), v((8, 256, PATCH), F32), v((8, 256, PATCH), F32),
                  v((8, 256, PATCH), BF16), v((8, 256, PATCH), BF16), v((HEADS, PATCH), F32), v((CLS, 3 * D), F32),
                  v((CLS, D), F32), v((CLS, 3 * D), F32), v((PATCH, 3 * D), BF16), v((3, PATCH, D), F32))

    def outcome(mid, hid, w_down, turn, flat, res):
        got_mid = load(3, mid_h, mid)

        def fetch(pair):
            copies = []
            for k in range(2):
                j = 2 * pair + k
                slot = pair % 2
                piece, t = relative(3 - j % 4), j // 4
                src = hid_h.at[k] if pair == 0 else hidden_o.at[j - 2]
                copies.append(pltpu.make_async_copy(src, hid.at[slot, :, pl.ds(k * TILE, TILE)], wsem.at[0, 2 * slot + k]))
                copies.append(pltpu.make_async_copy(full_down.at[piece, pl.ds(t * TILE, TILE), :],
                                                    w_down.at[slot, pl.ds(k * TILE, TILE), :], wsem.at[1, 2 * slot + k]))
            return copies

        for copy in fetch(0):
            copy.start()
        steps = {0: [lambda: red.on_z(cq[0]), lambda: red.on_x(cq[1])], 1: [lambda: red.on_back(cq[0])],
                 2: [lambda: red.on_y(cq[2]), lambda: red.on_z(cq[1])], 3: [lambda: red.on_back(cq[1])]}
        for pair in range(4):
            if pair < 3:
                for copy in fetch(pair + 1):
                    copy.start()
            for copy in fetch(pair):
                copy.wait()
            for q in range(2):
                cols = slice(q * TILE, (q + 1) * TILE)
                out = dot(hid[pair % 2], w_down[pair % 2, :, cols])
                if pair:
                    gmid[:, cols] += out
                else:
                    gmid[:, cols] = out
            for step in steps.get(pair, []):
                step()
        got_mid.wait()

        def rows_of(rows):
            projected = gmid[rows, :] + vecf[6:7, :]
            upstream = up_s[rows, :].astype(F32)
            acc[6] += fold(upstream * vecf[7:8, :])
            acc[7] += fold(upstream * projected)
            res[rows, :] = (mid[rows, :] + vecf[7:8, :] * projected).astype(BF16)

        rows_loop(n, 16, rows_of)
        for p in range(4):
            for k in range(8):
                v_part[p, k : k + 1, :] = jnp.sum(acc[k, :, p * 256 : (p + 1) * 256], axis=0, keepdims=True)
            joint = acc.at[8 + p // 2]
            for k in range(2):
                start = (p % 2) * TILE + k * 256
                v_part[p, 8 + k : 9 + k, :] = jnp.sum(joint[:, start : start + 256], axis=0, keepdims=True)
            for k in range(4):
                v_part[p, 10 + k : 11 + k, :] = sums_up[2 * p + k // 2 : 2 * p + k // 2 + 1, (k % 2) * 256 : (k % 2 + 1) * 256]
            v_part[p, 14:16, :] = jnp.zeros((2, 256), F32)
        for k in range(1, 4):
            group_copy(k).start()
        red.on_x(cq[2])
        total = v_part[s]
        for k in range(1, 4):
            group_copy(k).wait_recv()
            total = total + v_group[k - 1]
        v_sum[...] = total
        v_all[red.r] = total
        for k in range(1, 2 * nz):
            all_copy(k).start()
        to_tokens(res, flat, turn)
        copy = pltpu.make_async_copy(flat, result_o, osem.at[0])
        copy.start()
        red.on_z(cq[2])
        for k in range(1, 2 * nz):
            all_copy(k).wait_recv()
        total = v_all[0]
        for k in range(1, 2 * nz):
            total = total + v_all[k]
        v_group[0] = total
        small = pltpu.make_async_copy(v_group.at[0], small_o, osem.at[1])
        small.start()
        red.on_back(cq[2])
        copy.wait()
        small.wait()

    pl.run_scoped(outcome, v((n, D), F32), v((2, n, D), BF16), v((2, D, D), BF16), v((2, main, 128), F32),
                  v((main + images, D), BF16), v((n, D), BF16))
    copies = []
    for c in chunks:
        red.finish(c)
        half = c.rows // 2
        for k, (src, first, where) in enumerate(((x_recv, c.x_recv, red.x), (buf, c.far, 1 - red.x))):
            copy = pltpu.make_async_copy(
                src.at[pl.ds(first, half), :],
                sums_o.at[pl.ds(pl.multiple_of(c.mine - cd0.mine + where * half, 16), half), :], fsem.at[2 * c.index + k])
            copy.start()
            copies.append(copy)
    red.core_copy(6, 1024).wait_send()
    red.core_copy(7, 1024).wait_send()
    for k in range(1, 4):
        group_copy(k).wait_send()
    for k in range(1, 2 * nz):
        all_copy(k).wait_send()
    for c in chunks:
        red.drain(c)
    for copy in copies:
        copy.wait()


def convert_kernel(
    chunks, sums, small, result, tokens, result_o, tokens_o, g1_o, s1_o, qkv_o, bqv_o, out_o, bo_o, l1_o, g2_o, s2_o, up_o, bup_o, down_o, bd_o, l2_o,
    low, qkv, out, up, down, moved, dsem, osem, msem,
):
    base = chunks[0].mine
    moves = [pltpu.make_async_copy(src, moved.at[k], msem.at[0, k]) for k, src in enumerate((result, tokens))]
    stores = [pltpu.make_async_copy(moved.at[k], dst, msem.at[1, k]) for k, dst in enumerate((result_o, tokens_o))]
    gots = []
    for c in chunks:
        rows = pl.ds(c.mine - base, c.rows)
        gots.append(pltpu.make_async_copy(sums.at[rows, :], low.at[rows, :], dsem.at[c.index]))
        gots[-1].start()
    for copy in moves:
        copy.start()
    outs = []

    def send_out(src, dst):
        copy = pltpu.make_async_copy(src, dst, osem.at[len(outs)])
        copy.start()
        outs.append(copy)

    def block(c, first, count):
        return low[c.mine - base + first : c.mine - base + first + count, :]

    for t in range(2):
        gots[2 * t].wait()
        for k in range(8):
            down[t * TILE : (t + 1) * TILE, k * 128 : (k + 1) * 128] = block(chunks[2 * t], k * 128, 128).T.astype(F32)
        send_out(down.at[pl.ds(t * TILE, TILE), :], down_o.at[pl.ds(t * TILE, TILE), :])
        moves[t].wait()
        stores[t].start()
        gots[2 * t + 1].wait()
        up[t] = block(chunks[2 * t + 1], 0, D).astype(F32)
        send_out(up.at[t], up_o.at[:, pl.ds(t * TILE, TILE)])
    gots[4].wait()
    for k in range(2):
        out[:, k * TILE : (k + 1) * TILE] = block(chunks[4], k * 256, 256).astype(F32)
    send_out(out, out_o)
    for k in range(5, 8):
        gots[k].wait()
    for k in range(6):
        qkv[:, k * TILE : (k + 1) * TILE] = block(chunks[5], k * 256, 256).astype(F32)
    send_out(qkv, qkv_o)
    vectors = (g1_o, s1_o, bo_o, l1_o, g2_o, s2_o, bd_o, l2_o, bqv_o, bup_o)
    row = 0
    for v in vectors:
        for k in range(v.shape[0] // 256):
            v[pl.ds(k * 256, 256)] = small[row : row + 1, :].reshape(256)
            row += 1
    for copy in outs + stores:
        copy.wait()


def convert(chunks, sums, small, result, tokens):
    one = lambda k: jax.ShapeDtypeStruct((k,), F32)
    outs = (
        low_shape(*result.shape), low_shape(*tokens.shape), one(256), one(256), wide_shape(256, 3 * D), one(512), wide_shape(256, D), one(256), one(256), one(256), one(256),
        wide_shape(D, D), one(1024), wide_shape(D, D), one(256), one(256),
    )
    v = pltpu.VMEM
    return pl.pallas_call(
        functools.partial(convert_kernel, chunks),
        out_shape=outs,
        in_specs=[ANY, VMEM, ANY, ANY],
        out_specs=[VMEM if len(o.shape) == 1 else ANY for o in outs],
        scratch_shapes=[v(sums.shape, BF16), v((256, 3 * D), F32), v((256, D), F32), v((2, D, TILE), F32),
                        v((D, D), F32), v((2,) + result.shape, BF16), pltpu.SemaphoreType.DMA((8,)),
                        pltpu.SemaphoreType.DMA((6,)), pltpu.SemaphoreType.DMA((2, 2))],
        compiler_params=pltpu.CompilerParams(vmem_limit_bytes=LIMIT),
        name="gradients_to_float32",
    )(sums, small, result, tokens)


def low_shape(*shape):
    return jax.ShapeDtypeStruct(shape, BF16)


def wide_shape(*shape):
    return jax.ShapeDtypeStruct(shape, F32)


ANY = pl.BlockSpec(memory_space=pl.ANY)
VMEM = pl.BlockSpec(memory_space=pltpu.VMEM)
LIMIT = 62 * 2**20


def forward(flat, cot, vectors, w_qkv, w_out, w_up, w_down):
    images = flat.shape[0] // (PATCH + 1)
    n = images * PATCH + CLS
    v = pltpu.VMEM
    outs = (
        low_shape(D, 3 * D), low_shape(D, D), low_shape(4, D, D), low_shape(4, D, D), low_shape(4, 16, 256),
        low_shape(n, 3 * D), low_shape(D, n), low_shape(n, D), low_shape(D, n), wide_shape(n, D), low_shape(n, D),
        low_shape(n, D), low_shape(D, n), low_shape(n, D), low_shape(n, D), low_shape(D, n),
        wide_shape(images, HEADS, PATCH), wide_shape(images, HEADS, PATCH),
        low_shape(2, 2048, TILE), low_shape(2, n, TILE), wide_shape(n, D), wide_shape(8, TILE),
    )
    return pl.pallas_call(
        gather_kernel,
        out_shape=outs,
        in_specs=[VMEM] * 12 + [ANY] * 4,
        out_specs=[ANY] * len(outs),
        scratch_shapes=[
            v((D, 3 * D), BF16), v((D, D), BF16), v((4, D, D), BF16), v((4, D, D), BF16),
            v((n, D), BF16), v((n, 3 * D), BF16), v((n, D), BF16), v((n, D), BF16), v((n, D), F32), v((n, D), BF16),
            v((n, D), BF16), v((D, n), BF16), v((D, n), BF16),
            v((images, HEADS, PATCH), F32), v((images, HEADS, PATCH), F32),
            v((8, 256, PATCH), F32), v((8, 256, PATCH), BF16), v((PATCH, D), F32), v((HEADS, PATCH), F32),
            v((CLS, D), F32), v((CLS, 3 * D), F32), v((2, images * PATCH, 128), F32), v((16, 256), F32),
            v((16, 256), BF16), v((4, 16, 256), BF16), v((16, D), F32), v((8, 3 * D), F32), v((8, TILE), F32),
            v((8, TILE), F32), pltpu.SemaphoreType.DMA((2, 7, 11)), pltpu.SemaphoreType.DMA((7,)), pltpu.SemaphoreType.DMA((2, 3)),
            pltpu.SemaphoreType.DMA((30,)),
        ],
        compiler_params=pltpu.CompilerParams(collective_id=0, has_side_effects=True, vmem_limit_bytes=LIMIT),
        cost_estimate=pl.CostEstimate(flops=18 * 2**30, bytes_accessed=64 * 2**20, transcendentals=3 * 2**20),
        name="gather_and_attention",
    )(flat, cot, *vectors, w_qkv, w_out, w_up, w_down)


def backward(nz, images, vec, *arrays):
    n = images * PATCH + CLS
    tokens = images * (PATCH + 1)
    v = pltpu.VMEM
    chunks, sizes = chunk_layout(nz)
    outs = (low_shape(tokens, D), low_shape(tokens, D), low_shape(sizes["total"], TILE), wide_shape(16, 256),
            low_shape(6, n, TILE))
    return pl.pallas_call(
        functools.partial(backward_kernel, nz, chunks),
        out_shape=outs,
        in_specs=[VMEM] + [ANY] * len(arrays),
        out_specs=[ANY] * len(outs),
        scratch_shapes=[
            v((sizes["buf"], TILE), BF16), v((2, 2048, TILE), BF16), v((sizes["y_recv"], TILE), BF16),
            v((sizes["x_recv"], TILE), BF16), v((nz - 1, sizes["z_recv"], TILE), BF16), v((n, D), F32), v((n, D), F32), v((n, D), BF16),
            v((10, 8, D), F32), v((8, TILE), F32), v((16, D), F32), v((8, 3 * D), F32), v((8, TILE), F32),
            v((4, 16, 256), F32), v((3, 16, 256), F32), v((16, 256), F32), v((2 * nz, 16, 256), F32),
            pltpu.SemaphoreType.DMA((2, len(chunks), 3 * nz)), pltpu.SemaphoreType.DMA((2, 8)),
            pltpu.SemaphoreType.DMA((2, 3)), pltpu.SemaphoreType.DMA((2, 2 * nz - 1)),
            pltpu.SemaphoreType.REGULAR, pltpu.SemaphoreType.DMA((12,)), pltpu.SemaphoreType.DMA((2, 4)),
            pltpu.SemaphoreType.DMA((2,)), pltpu.SemaphoreType.DMA((2,)), pltpu.SemaphoreType.DMA((2 * len(chunks),)),
        ],
        compiler_params=pltpu.CompilerParams(collective_id=1, has_side_effects=True, vmem_limit_bytes=LIMIT),
        cost_estimate=pl.CostEstimate(flops=66 * 2**30, bytes_accessed=128 * 2**20, transcendentals=8 * 2**20),
        name="layer_backward",
    )(vec, *arrays), chunks


def on_device(
    tokens, norm1_gain, norm1_shift, w_qkv, bias_qv, w_out, bias_out, scale_one, norm2_gain, norm2_shift, w_up, bias_up,
    w_down, bias_down, scale_two, cotangent,
):
    images, length, _ = tokens.shape
    nz = lax.axis_size("replica") // 2
    flatten = lambda a: jnp.transpose(a, (1, 0, 2)).reshape(images * length, D)
    restore = lambda a: jnp.transpose(a.reshape(length, images, D), (1, 0, 2))
    vectors = (norm1_gain, norm1_shift, bias_out, scale_one, norm2_gain, norm2_shift, bias_down, scale_two, bias_qv, bias_up)
    full_qkv, full_out, full_up, full_down, vec, *kept = forward(
        flatten(tokens), flatten(cotangent), vectors, w_qkv, w_out, w_up, w_down)
    (result, grad_tokens, sums, small, _), chunks = backward(nz, images, vec, full_qkv, full_out, full_up, full_down, *kept)
    result, grad_tokens, *gradients = convert(chunks, sums, small, result, grad_tokens)
    return (restore(result), restore(grad_tokens)) + tuple(gradients)


def solution(mesh):
    placed = (
        P(("shard", "replica"), None, None),
        P("shard"),
        P("shard"),
        P("shard", None),
        P("shard"),
        P("shard", None),
        P("shard"),
        P("shard"),
        P("shard"),
        P("shard"),
        P(None, "shard"),
        P("shard"),
        P("shard", None),
        P("shard"),
        P("shard"),
        P(("shard", "replica"), None, None),
    )
    return jax.shard_map(
        on_device,
        mesh=mesh,
        in_specs=placed,
        out_specs=(
            P(("shard", "replica"), None, None),
            P(("shard", "replica"), None, None),
            P("shard"),
            P("shard"),
            P("shard", None),
            P("shard"),
            P("shard", None),
            P("shard"),
            P("shard"),
            P("shard"),
            P("shard"),
            P(None, "shard"),
            P("shard"),
            P("shard", None),
            P("shard"),
            P("shard"),
        ),
        check_vma=False,
    )
```

profile of v0, /device:TPU:2, one launch (start us, length us, event | category | flops | bytes accessed | tf_op | source)
XLA Modules:
  0.0 321.7 jit_solution(12370758510684988942)
XLA Ops:
  0.7 93.1 %gather_and_attention.1 = (bf16[1024,3072]{1,0:T(8,128)(2,1)}, bf16[1024,1024]{1,0:T(8,128)(2,1)}, bf16[4,1024,1024]{2,1,0:T(8,128)(2,1)}, bf16[4,1024,1024]{2,1...) custom-call(bf16[1032,1024]{1,0:T(8,128)(2,1)} %bitcast.12, ...), custom_call_target="tpu_custom_call" | custom-call | flops 19327352832 | bytes 67108864 | tf_op jit(solution)/shard_map/gather_and_attention/pallas_call | solution.py:1267
  93.7 216.5 %layer_backward.1 = (bf16[1032,1024]{1,0:T(8,128)(2,1)}, bf16[1032,1024]{1,0:T(8,128)(2,1)}, bf16[6144,512]{1,0:T(8,128)(2,1)}, f32[16,256]{1,0:T(8,128)}, bf16[6,1040,512]{2,1,0:T(8,128)(2,1)}) custom-call(bf16[4,16,256]{2,1,0:T(8,128)(2,1)} %get-tuple-element.58.vec, bf16[1024,3072]{1,0:T(8,128)(2,1)} %get-tuple-element.59.full_qkv, ...), custom_call_target="tpu_custom_call" | custom-call | flops 70866960384 | bytes 134217728 | tf_op jit(solution)/shard_map/layer_backward/pallas_call | solution.py:1296
  310.2 11.0 %gradients_to_float32.1 = (bf16[1032,1024]{1,0:T(8,128)(2,1)}, bf16[1032,1024]{1,0:T(8,128)(2,1)}, f32[256]{0:T(256)}, f32[256]{0:T(256)}, f32[256,3072]{1,0:T(8...) custom-call(bf16[6144,512]{1,0:T(8,128)(2,1)} %get-tuple-element.80., ...), custom_call_target="tpu_custom_call" | custom-call | tf_op jit(solution)/shard_map/gradients_to_float32/pallas_call | solution.py:1230
where the time goes:
time: 328 us; the launch traced here: 322 us
  Pallas kernels  321 us (98%)
    pallas_call x1, Pallas kernels, backward(): pl.pallas_call(functools.partial(backward_kernel, nz, chunks), out_shape=...  216 us
    pallas_call x1, Pallas kernels, forward(): pl.pallas_call(gather_kernel, out_shape=outs, in_specs=[VMEM] * 12 + [ANY...  93.1 us
    pallas_call x1, Pallas kernels, convert(): pl.pallas_call(functools.partial(convert_kernel, chunks), out_shape=outs,...  11 us

commit v1 on v0

--- a/solution.py
+++ b/solution.py
@@ -286,13 +286,13 @@
 
 
 def gather_kernel(
-    tokens, cot, v0, v1, v2, v3, v4, v5, v6, v7, v8, v9, w_qkv, w_out, w_up, w_down,
+    tokens_h, cot_h, v0, v1, v2, v3, v4, v5, v6, v7, v8, v9, w_qkv, w_out, w_up, w_down,
     qkv_w_o, out_w_o, up_w_o, down_w_o, vec_all, qkv_o, act_t_o, x_o, att_t_o, mid_o, branch_o, act2_o, act2_t_o, up_o,
     dr_o, dr_t_o, lse_o, lsec_o, parts_o, hid_o, gact_o, column_o,
     full_qkv, full_out, full_up, full_down, x_s, qkv, act, att, mid, branch, act2, turned_a, turned_b, lse, lsec,
     scores, probs, mix, probs_cls, cls, qkv_cls, turn, vec32, vec_own_s, vec, vecf, bias_qkv,
-    bias_up, column,
-    sems, local, vsem, osem,
+    bias_up, column, core_in, flat,
+    sems, local, vsem, osem, csem, fsem,
 ):
     s, r, x, z = place()
     sib, across, side = peers(s, r)
@@ -300,6 +300,12 @@
     images = lse.shape[0]
     main = images * PATCH
 
+    def load(src):
+        copy = pltpu.make_async_copy(src, flat, fsem.at[0])
+        copy.start()
+        return copy
+
+    got_tokens = load(tokens_h)
     vec32[...] = jnp.zeros_like(vec32)
     pack_vectors((v0, v1, v2, v3, v4, v5, v6, v7, v8, v9), vec32)
     vec_own_s[...] = vec32[...].astype(BF16)
@@ -350,7 +356,9 @@
     g_out.begin()
     vec[s] = vec_own_s[...]
 
-    to_images(tokens, x_s, turn)
+    got_tokens.wait()
+    to_images(flat, x_s, turn)
+    got_cot = load(cot_h)
     outs = {}
 
     def send_out(k, src, dst):
@@ -375,7 +383,8 @@
         g.begin()
     transpose_into(act, turned_b)
     send_out(1, turned_b, act_t_o)
-    to_images(cot, branch, turn)
+    got_cot.wait()
+    to_images(flat, branch, turn)
     g_qa.on_last()
     g_qb.on_near()
 
@@ -464,6 +473,11 @@
     for k in (2, 11):
         outs.pop(k).wait()
     hid, br = qkv.at[:, pl.ds(0, TILE)], qkv.at[:, pl.ds(TILE, TILE)]
+    def core_copy(half_k):
+        return pltpu.make_async_remote_copy(
+            qkv.at[pl.ds(0, D), pl.ds((2 + half_k) * TILE, TILE)], core_in.at[half_k], csem.at[0, half_k],
+            csem.at[1, half_k], device_id={"shard": sib}, device_id_type=MESH)
+
     for k, rel in enumerate((3, 2)):
         piece = relative_piece(s, rel)
 
@@ -475,17 +489,29 @@
         column[pl.ds(2 * piece, 1), :] = ffn_tile(
             act2, act, turned_a, turned_b, lambda: full_up[piece, :, 0:TILE], lambda: full_down[piece, 0:TILE, :],
             bias_up[pl.ds(2 * piece, 1), :], hid, br, mid, k == 0, lambda: None, lambda: send_out(22 + k, hid, hid_o.at[k]), put)
-        for half_k in range(2):
-            send_out(24 + 2 * k + half_k, qkv.at[pl.ds(0, D), pl.ds((2 + 2 * k + half_k) * TILE, TILE)],
-                     parts_o.at[k, pl.ds(half_k * D, D), :])
         if k == 0:
+            for half_k in range(2):
+                core_copy(half_k).start()
             g_down1.on_last()
             g_up1.ready()
             send_out(20, full_up.at[:, :, rest], up_w_o.at[:, :, rest])
     send_out(28, mid, gact_o)
+    for half_k in range(2):
+        core_copy(half_k).wait_recv()
+        cols = slice((4 + half_k) * TILE, (5 + half_k) * TILE)
+
+        def join(k, carry, half_k=half_k, cols=cols):
+            rows = at(k, 128)
+            qkv[rows, cols] = (qkv[rows, cols].astype(F32) + core_in[half_k, rows, :].astype(F32)).astype(BF16)
+            return carry
+
+        lax.fori_loop(0, D // 128, join, 0)
+        send_out(24 + half_k, qkv.at[pl.ds(0, D), pl.ds((4 + half_k) * TILE, TILE)], parts_o.at[pl.ds(half_k * D, D), :])
     send_out(29, column, column_o)
     g_down1.ready()
     send_out(21, full_down.at[:, rest, :], down_w_o.at[:, rest, :])
+    for half_k in range(2):
+        core_copy(half_k).wait_send()
     for copy in outs.values():
         copy.wait()
     for g in (g_qa, g_qb, g_out, g_up0, g_down0, g_up1, g_down1):
@@ -800,11 +826,10 @@
 
         for copy in fetch(2, 0):
             copy.start()
-        got_parts, got_act2, got_dr = (load(8, parts_h.at[0], buf.at[pl.ds(0, 2048), :]), load(0, act2_h, act2),
+        got_parts, got_act2, got_dr = (load(8, parts_h, buf.at[pl.ds(cd0.y_send, 2048), :]), load(0, act2_h, act2),
                                        load(1, dr_h, dr))
         got_gact, got_column = load(10, gact_h, gmid), load(11, column_h, sums_up)
-        gots = [got_parts, load(9, parts_h.at[1], buf.at[pl.ds(cd0.y_send, 2048), :]), got_act2, got_dr,
-                load(2, dr_t_h, dr_t), load(3, act2_t_h, act2_t), got_gact, got_column]
+        late = [load(2, dr_t_h, dr_t), load(3, act2_t_h, act2_t)]
 
         def keep(j, slot):
             return pltpu.make_async_copy(hid.at[slot], hidden_o.at[j - 2], hsem.at[slot])
@@ -817,11 +842,11 @@
         unpack_vectors(vec, vecf, bias_qkv)
         unpack_bias_up(vec, bias_up)
         acc[...] = jnp.zeros_like(acc)
-        gots[0].wait()
-        red.core_copy(0, 2048).start()
-        late = gots[4:6]
-        for copy in gots[2:4]:
-            copy.wait()
+        got_parts.wait()
+        red.y_copy(cd0).start()
+        red.y_copy(cu0).start()
+        got_act2.wait()
+        got_dr.wait()
 
         def tile(j, carry):
             slot = lax.rem(j, 2)
@@ -842,7 +867,7 @@
             def _():
                 keep(j - 2, slot).wait()
 
-            for k in (2, 4, 6):
+            for k in (4, 6):
                 @pl.when(j == k)
                 def _(k=k):
                     red.core_copy(k // 2 - 1, 2048).wait_send()
@@ -850,7 +875,7 @@
             def on_back():
                 @pl.when(j == 2)
                 def _():
-                    for copy in gots[1:2] + gots[6:]:
+                    for copy in (got_gact, got_column):
                         copy.wait()
 
             def on_hidden():
@@ -879,12 +904,12 @@
                 red.add_core(turn, 0, chunk[0].mine, 2048)
 
             steps = {
-                2: [lambda: y_part(0, (cd0, cu0)), lambda: red.core_copy(1, 2048).start()],
+                2: [lambda: red.core_copy(1, 2048).start()],
                 3: [lambda: own_part(1, (cd0, cu0))],
-                4: [lambda: red.core_copy(2, 2048).start()],
-                5: [lambda: y_part(2, (cd1, cu1)), lambda: red.on_y(cd0)],
-                6: [lambda: red.core_copy(3, 2048).start(), lambda: red.on_x(cd0)],
-                7: [lambda: own_part(3, (cd1, cu1)), lambda: red.on_y(cu0)],
+                4: [lambda: red.core_copy(2, 2048).start(), lambda: red.on_y(cd0)],
+                5: [lambda: y_part(2, (cd1, cu1))],
+                6: [lambda: red.core_copy(3, 2048).start(), lambda: red.on_x(cd0), lambda: red.on_y(cu0)],
+                7: [lambda: own_part(3, (cd1, cu1))],
             }
             for k, todo in steps.items():
                 @pl.when(j == k)
@@ -948,6 +973,7 @@
                 brr[rows, :] = gb.astype(BF16)
 
             rows_loop(n, 16, norm_rows)
+            red.on_x(cu0)
             got_att.wait()
             for q in range(2):
                 spread(dot(att_t[...], brr[:, q * TILE : (q + 1) * TILE]), co, q * 256, 4)
@@ -955,7 +981,6 @@
             got_out.wait()
             for q in range(2):
                 datt[:, q * TILE : (q + 1) * TILE] = dot_nt(brr[...], w_out[q * TILE : (q + 1) * TILE, :]).astype(BF16)
-            red.on_x(cu0)
 
         pl.run_scoped(middle, v((n, D), F32), v((n, D), BF16), v((D, n), BF16), v((D, D), BF16))
         got_qkv.wait()
@@ -966,8 +991,8 @@
         joint_cls[...] = jnp.zeros_like(joint_cls)
         pl.semaphore_wait(credit, 1)
         on_core(4, co)
-        plan = {0: [lambda: red.on_y(cd1), lambda: red.on_back(cd0)], 3: [lambda: red.on_z(cu0)], 5: [lambda: red.on_x(cd1)],
-                6: [lambda: red.on_y(cu1), lambda: red.on_back(cu0)]}
+        plan = {0: [lambda: red.on_y(cd1), lambda: red.on_back(cd0)], 1: [lambda: red.on_z(cu0)],
+                3: [lambda: red.on_x(cd1), lambda: red.on_back(cu0)], 5: [lambda: red.on_y(cu1)], 6: [lambda: red.on_z(cd1)]}
 
         def image(i, carry):
             for k, steps in plan.items():
@@ -1008,7 +1033,7 @@
             got_act.wait()
             weight_grad(0)
             red.core_copy(5, 1024).start()
-            red.on_z(cd1)
+            red.on_x(cu1)
             red.core_copy(4, 1024).wait_send()
             weight_grad(1)
             on_core(5, cq[0])
@@ -1018,16 +1043,15 @@
             weight_grad(2)
             on_core(6, cq[1])
             red.core_copy(7, 1024).start()
-            red.on_x(cu1)
             red.on_back(cd1)
             input_grad(0)
+            red.on_z(cu1)
             input_grad(1)
             on_core(7, cq[2])
             red.on_x(co)
             input_grad(2)
             red.on_y(cq[0])
             input_grad(3)
-            red.on_z(cu1)
             got_x.wait()
 
             def norm_rows(rows):
@@ -1262,12 +1286,12 @@
         low_shape(n, 3 * D), low_shape(D, n), low_shape(n, D), low_shape(D, n), wide_shape(n, D), low_shape(n, D),
         low_shape(n, D), low_shape(D, n), low_shape(n, D), low_shape(n, D), low_shape(D, n),
         wide_shape(images, HEADS, PATCH), wide_shape(images, HEADS, PATCH),
-        low_shape(2, 2048, TILE), low_shape(2, n, TILE), wide_shape(n, D), wide_shape(8, TILE),
+        low_shape(2048, TILE), low_shape(2, n, TILE), wide_shape(n, D), wide_shape(8, TILE),
     )
     return pl.pallas_call(
         gather_kernel,
         out_shape=outs,
-        in_specs=[VMEM] * 12 + [ANY] * 4,
+        in_specs=[ANY] * 2 + [VMEM] * 10 + [ANY] * 4,
         out_specs=[ANY] * len(outs),
         scratch_shapes=[
             v((D, 3 * D), BF16), v((D, D), BF16), v((4, D, D), BF16), v((4, D, D), BF16),
@@ -1277,8 +1301,9 @@
             v((8, 256, PATCH), F32), v((8, 256, PATCH), BF16), v((PATCH, D), F32), v((HEADS, PATCH), F32),
             v((CLS, D), F32), v((CLS, 3 * D), F32), v((2, images * PATCH, 128), F32), v((16, 256), F32),
             v((16, 256), BF16), v((4, 16, 256), BF16), v((16, D), F32), v((8, 3 * D), F32), v((8, TILE), F32),
-            v((8, TILE), F32), pltpu.SemaphoreType.DMA((2, 7, 11)), pltpu.SemaphoreType.DMA((7,)), pltpu.SemaphoreType.DMA((2, 3)),
-            pltpu.SemaphoreType.DMA((30,)),
+            v((8, TILE), F32), v((2, D, TILE), BF16), v(flat.shape, BF16), pltpu.SemaphoreType.DMA((2, 7, 11)), pltpu.SemaphoreType.DMA((7,)), pltpu.SemaphoreType.DMA((2, 3)),
+            pltpu.SemaphoreType.DMA((30,)), pltpu.SemaphoreType.DMA((2, 2)),
+            pltpu.SemaphoreType.DMA((1,)),
         ],
         compiler_params=pltpu.CompilerParams(collective_id=0, has_side_effects=True, vmem_limit_bytes=LIMIT),
         cost_estimate=pl.CostEstimate(flops=18 * 2**30, bytes_accessed=64 * 2**20, transcendentals=3 * 2**20),

time: 328 us -> 322 us (0.982)
  the two profiles are of different devices: /device:TPU:2 before, /device:TPU:0 now
where the time goes in v1:
time: 322 us; the launch traced here: 318 us
  Pallas kernels  317 us (98%)
    pallas_call x1, Pallas kernels, backward(): pl.pallas_call(functools.partial(backward_kernel, nz, chunks), out_shape=...  213 us
    pallas_call x1, Pallas kernels, forward(): pl.pallas_call(gather_kernel, out_shape=outs, in_specs=[ANY] * 2 + [VMEM]...  92.9 us
    pallas_call x1, Pallas kernels, convert(): pl.pallas_call(functools.partial(convert_kernel, chunks), out_shape=outs,...  11 us

profile of v1, /device:TPU:0, one launch (start us, length us, event | category | flops | bytes accessed | tf_op | source)
XLA Modules:
  0.0 318.0 jit_solution(2982587555434263217)
XLA Ops:
  0.7 92.9 %gather_and_attention.1 = (bf16[1024,3072]{1,0:T(8,128)(2,1)}, bf16[1024,1024]{1,0:T(8,128)(2,1)}, bf16[4,1024,1024]{2,1,0:T(8,128)(2,1)}, bf16[4,1024,1024]{2,1...) custom-call(bf16[1032,1024]{1,0:T(8,128)(2,1)} %bitcast.12, ...), custom_call_target="tpu_custom_call" | custom-call | flops 19327352832 | bytes 67108864 | tf_op jit(solution)/shard_map/gather_and_attention/pallas_call | solution.py:1291
  93.6 213.0 %layer_backward.1 = (bf16[1032,1024]{1,0:T(8,128)(2,1)}, bf16[1032,1024]{1,0:T(8,128)(2,1)}, bf16[6144,512]{1,0:T(8,128)(2,1)}, f32[16,256]{1,0:T(8,128)}, bf16[6,1040,512]{2,1,0:T(8,128)(2,1)}) custom-call(bf16[4,16,256]{2,1,0:T(8,128)(2,1)} %get-tuple-element.58.vec, bf16[1024,3072]{1,0:T(8,128)(2,1)} %get-tuple-element.59.full_qkv, ...), custom_call_target="tpu_custom_call" | custom-call | flops 70866960384 | bytes 134217728 | tf_op jit(solution)/shard_map/layer_backward/pallas_call | solution.py:1321
  306.5 11.0 %gradients_to_float32.1 = (bf16[1032,1024]{1,0:T(8,128)(2,1)}, bf16[1032,1024]{1,0:T(8,128)(2,1)}, f32[256]{0:T(256)}, f32[256]{0:T(256)}, f32[256,3072]{1,0:T(8...) custom-call(bf16[6144,512]{1,0:T(8,128)(2,1)} %get-tuple-element.80., ...), custom_call_target="tpu_custom_call" | custom-call | tf_op jit(solution)/shard_map/gradients_to_float32/pallas_call | solution.py:1254

commit v2 on v1

--- a/solution.py
+++ b/solution.py
@@ -878,6 +878,11 @@
                     for copy in (got_gact, got_column):
                         copy.wait()
 
+                for k, chunk in ((4, cd0), (6, cu0)):
+                    @pl.when(j == k)
+                    def _(chunk=chunk):
+                        red.on_y(chunk)
+
             def on_hidden():
                 keep(j, slot).start()
 
@@ -906,9 +911,9 @@
             steps = {
                 2: [lambda: red.core_copy(1, 2048).start()],
                 3: [lambda: own_part(1, (cd0, cu0))],
-                4: [lambda: red.core_copy(2, 2048).start(), lambda: red.on_y(cd0)],
-                5: [lambda: y_part(2, (cd1, cu1))],
-                6: [lambda: red.core_copy(3, 2048).start(), lambda: red.on_x(cd0), lambda: red.on_y(cu0)],
+                4: [lambda: red.core_copy(2, 2048).start()],
+                5: [lambda: y_part(2, (cd1, cu1)), lambda: red.on_x(cd0)],
+                6: [lambda: red.core_copy(3, 2048).start()],
                 7: [lambda: own_part(3, (cd1, cu1))],
             }
             for k, todo in steps.items():
@@ -951,6 +956,7 @@
             got_mid, got_branch = load(3, mid_h, mid), load(4, branch_h, branch)
             got_att, got_out = load(5, att_t_h, att_t), load(6, full_out, w_out)
             red.on_z(cd0)
+            red.on_x(cu0)
             got_mid.wait()
             got_branch.wait()
 
@@ -973,7 +979,6 @@
                 brr[rows, :] = gb.astype(BF16)
 
             rows_loop(n, 16, norm_rows)
-            red.on_x(cu0)
             got_att.wait()
             for q in range(2):
                 spread(dot(att_t[...], brr[:, q * TILE : (q + 1) * TILE]), co, q * 256, 4)
@@ -991,7 +996,7 @@
         joint_cls[...] = jnp.zeros_like(joint_cls)
         pl.semaphore_wait(credit, 1)
         on_core(4, co)
-        plan = {0: [lambda: red.on_y(cd1), lambda: red.on_back(cd0)], 1: [lambda: red.on_z(cu0)],
+        plan = {0: [lambda: red.on_y(cd1)], 1: [lambda: red.on_back(cd0)], 2: [lambda: red.on_z(cu0)],
                 3: [lambda: red.on_x(cd1), lambda: red.on_back(cu0)], 5: [lambda: red.on_y(cu1)], 6: [lambda: red.on_z(cd1)]}
 
         def image(i, carry):

time: 322 us -> 325 us (level)
  no operation moved by 1% of the time
where the time goes in v2:
time: 325 us; the launch traced here: 319 us
  Pallas kernels  318 us (98%)
    pallas_call x1, Pallas kernels, backward(): pl.pallas_call(functools.partial(backward_kernel, nz, chunks), out_shape=...  214 us
    pallas_call x1, Pallas kernels, forward(): pl.pallas_call(gather_kernel, out_shape=outs, in_specs=[ANY] * 2 + [VMEM]...  92.9 us
    pallas_call x1, Pallas kernels, convert(): pl.pallas_call(functools.partial(convert_kernel, chunks), out_shape=outs,...  11 us

profile of v2, /device:TPU:0, one launch (start us, length us, event | category | flops | bytes accessed | tf_op | source)
XLA Modules:
  0.0 319.4 jit_solution(5247892236799257228)
XLA Ops:
  0.7 92.9 %gather_and_attention.1 = (bf16[1024,3072]{1,0:T(8,128)(2,1)}, bf16[1024,1024]{1,0:T(8,128)(2,1)}, bf16[4,1024,1024]{2,1,0:T(8,128)(2,1)}, bf16[4,1024,1024]{2,1...) custom-call(bf16[1032,1024]{1,0:T(8,128)(2,1)} %bitcast.12, ...), custom_call_target="tpu_custom_call" | custom-call | flops 19327352832 | bytes 67108864 | tf_op jit(solution)/shard_map/gather_and_attention/pallas_call | solution.py:1296
  93.6 214.3 %layer_backward.1 = (bf16[1032,1024]{1,0:T(8,128)(2,1)}, bf16[1032,1024]{1,0:T(8,128)(2,1)}, bf16[6144,512]{1,0:T(8,128)(2,1)}, f32[16,256]{1,0:T(8,128)}, bf16[6,1040,512]{2,1,0:T(8,128)(2,1)}) custom-call(bf16[4,16,256]{2,1,0:T(8,128)(2,1)} %get-tuple-element.58.vec, bf16[1024,3072]{1,0:T(8,128)(2,1)} %get-tuple-element.59.full_qkv, ...), custom_call_target="tpu_custom_call" | custom-call | flops 70866960384 | bytes 134217728 | tf_op jit(solution)/shard_map/layer_backward/pallas_call | solution.py:1326
  307.9 11.0 %gradients_to_float32.1 = (bf16[1032,1024]{1,0:T(8,128)(2,1)}, bf16[1032,1024]{1,0:T(8,128)(2,1)}, f32[256]{0:T(256)}, f32[256]{0:T(256)}, f32[256,3072]{1,0:T(8...) custom-call(bf16[6144,512]{1,0:T(8,128)(2,1)} %get-tuple-element.80., ...), custom_call_target="tpu_custom_call" | custom-call | tf_op jit(solution)/shard_map/gradients_to_float32/pallas_call | solution.py:1259
